TPU v7x, 32 devices: a whole 2x2x4 slice. The times are simulated.
32 devices in a mesh: slab: 2 (over x), tile: 16 (over z, y, core).
Axes of the slice: x: 2, y: 2, z: 4, core: 2. Of those that a mesh axis runs over, the one named last changes fastest.
Arguments:
- estimate: float32 [256, 32, 128], P(('slab', 'tile')), parts along dimension 0, may hold values from 0.5 to 2
- observed: bfloat16 [8, 256, 32, 128], P(None, ('slab', 'tile')), parts along dimension 1, may hold values from 0.5 to 2
- interp: bfloat16 [8, 256, 32, 128], P(None, ('slab', 'tile')), parts along dimension 1, may hold values from 0 to 1
- source_rows: int32 [8, 256, 32], P(None, ('slab', 'tile')), parts along dimension 1, may hold values from 0 to 127, as said below
- tissue: int32 [256], P(('slab', 'tile')), parts along dimension 0, may hold values 0 or 1
- psf_x: float32 [8, 9], replicated, may hold values from 0.1 to 1
- psf_y: float32 [8, 9], replicated, may hold values from 0.1 to 1
- psf_z: float32 [8, 33], replicated, may hold values from 0.05 to 1
Outputs:
- refined: float32 [256, 32, 128], P(('slab', 'tile')), parts along dimension 0
There are 2 independent parts, one for each index of `slab`. A program takes and returns all parts, laid end to end along the dimension named above; an argument that names none is the same for every part. Nothing has to cross between parts.
Inputs may be any that keep to these rules, and one draw needn't show every extreme that they name: `source_rows`: for each view, among the 8 x 32 joining lines of one device at most 32 take their source row from the rows of any one device, and some device's lines reach 32 from one device.
All inputs are finite; a program needn't handle non-finite values. No bound on the sum of `tissue` on one device may be relied on, other than what follows from the above.
Results may differ from a plain program's by a relative error of at most 0.0014.
Values may be sent and summed in bfloat16 or wider, within the bound.
A program may use at most 64 MiB of HBM per device.

v0:
```python
import functools

import jax
import jax.numpy as jnp
from jax import lax
from jax.experimental import pallas as pl
from jax.experimental.pallas import tpu as pltpu
from jax.sharding import PartitionSpec as P


def extended_2(value, sides, width):
    for axis, dim in sides:
        size, length = (lax.axis_size(axis), value.shape[dim])
        up = [(i, (i + 1) % size) for i in range(size - 1)]
        down = [(j, i) for i, j in up]
        last = lax.slice_in_dim(value, length - width, length, axis=dim)
        first = lax.slice_in_dim(value, 0, width, axis=dim)
        before = lax.ppermute(last, axis, up)
        after = lax.ppermute(first, axis, down)
        value = jnp.concatenate([before, value, after], axis=dim)
    return value


def taps_matrix(coeffs, count):
    half_taps = coeffs.shape[0] // 2
    offsets = jnp.arange(count)[:, None] - jnp.arange(count)[None, :] + half_taps
    inside = (offsets >= 0) & (offsets < coeffs.shape[0])
    return jnp.where(inside, coeffs[jnp.clip(offsets, 0, coeffs.shape[0] - 1)], jnp.float32(0.0))


def forward_x(extended, coeffs, out_rows):
    result = coeffs[0] * extended[0:out_rows]
    for offset in range(1, coeffs.shape[0]):
        result = result + coeffs[offset] * extended[offset : offset + out_rows]
    return result


def adjoint_x(extended, coeffs, out_rows):
    half_taps = coeffs.shape[0] // 2
    result = jnp.zeros((out_rows,) + extended.shape[1:], jnp.float32)
    for offset in range(coeffs.shape[0]):
        start = 2 * half_taps - offset
        result = result + coeffs[offset] * extended[start : start + out_rows]
    return result


def forward_yz(volume, matrix_z, matrix_y):
    volume = jnp.einsum("xzy,zw->xwy", volume, matrix_z, precision=lax.Precision.HIGHEST)
    return jnp.einsum("xzy,yu->xzu", volume, matrix_y, precision=lax.Precision.HIGHEST)


def adjoint_yz(volume, matrix_z, matrix_y):
    volume = jnp.einsum("xzu,yu->xzy", volume, matrix_y, precision=lax.Precision.HIGHEST)
    return jnp.einsum("xwy,zw->xzy", volume, matrix_z, precision=lax.Precision.HIGHEST)


def body_by_collectives(estimate, observed, interp, source_rows, tissue, psf_x, psf_y, psf_z):
    tile_rows, depth_cells, lane_cells = estimate.shape
    view_count = observed.shape[0]
    tile_count = lax.axis_size("tile")
    line_count = tile_rows * depth_cells
    capacity = 2 * line_count // tile_count
    half_taps = psf_x.shape[1] // 2
    flat_obs = observed.reshape(view_count * line_count, lane_cells)
    owners = (source_rows // tile_rows).reshape(view_count, line_count)
    payload = (
        jnp.arange(view_count, dtype=jnp.int32)[:, None, None] * line_count
        + source_rows % tile_rows * depth_cells
        + jnp.arange(depth_cells, dtype=jnp.int32)[None, None, :]
    ).reshape(view_count, line_count)
    owner_hits = (
        owners[:, :, None] == jnp.arange(tile_count, dtype=jnp.int32)[None, None, :]
    ).astype(jnp.int32)
    slot_index = jnp.sum((jnp.cumsum(owner_hits, axis=1) - 1) * owner_hits, axis=2)
    view_column = jnp.broadcast_to(
        jnp.arange(view_count, dtype=jnp.int32)[:, None], (view_count, line_count)
    )
    requests = jnp.zeros((tile_count, view_count, capacity), jnp.int32)
    requests = requests.at[owners, view_column, slot_index].set(payload)
    returned = lax.all_to_all(
        flat_obs[lax.all_to_all(requests, "tile", split_axis=0, concat_axis=0, tiled=True)],
        "tile",
        split_axis=0,
        concat_axis=0,
        tiled=True,
    )
    gathered_lines = returned[owners, view_column, slot_index]
    extended = extended_2(estimate.astype(jnp.bfloat16), (("tile", 0),), half_taps).astype(
        estimate.dtype
    )
    running = jnp.zeros_like(estimate)
    for view in range(view_count):
        taps_x = psf_x[view] / jnp.sum(psf_x[view])
        taps_y = psf_y[view] / jnp.sum(psf_y[view])
        taps_z = psf_z[view] / jnp.sum(psf_z[view])
        matrix_z = taps_matrix(taps_z, depth_cells)
        matrix_y = taps_matrix(taps_y, lane_cells)
        view_lines = gathered_lines[view]
        source_line = view_lines.reshape(tile_rows, depth_cells, lane_cells).astype(jnp.float32)
        next_line = jnp.concatenate([source_line[..., 1:], source_line[..., -1:]], axis=2)
        weight = interp[view].astype(jnp.float32)
        joined_view = weight * source_line + (1.0 - weight) * next_line
        blurred = forward_yz(forward_x(extended, taps_x, tile_rows), matrix_z, matrix_y)
        quotient = joined_view / blurred
        corrected = adjoint_yz(quotient, matrix_z, matrix_y)
        corrected_band = extended_2(
            corrected.astype(jnp.bfloat16), (("tile", 0),), half_taps
        ).astype(corrected.dtype)
        running = running + adjoint_x(corrected_band, taps_x, tile_rows)
    updated = estimate * running / view_count
    return jnp.where(tissue[:, None, None] == 1, updated, estimate)


MESH = pl.DeviceIdType.MESH
F32 = jnp.float32
BF16 = jnp.bfloat16


def split(value):
    high = value.astype(BF16)
    return high, (value - high.astype(F32)).astype(BF16)


def dot(left, right):
    return jnp.dot(left, right, preferred_element_type=F32)


def dot_split(left, right):
    return dot(left[0], right[0]) + dot(left[0], right[1]) + dot(left[1], right[0])


def one_hot(mask):
    return jnp.where(mask, 1.0, 0.0).astype(BF16)


def sweep_kernel(
    n, est, obs, interp, rows, px, py, pz, out,
    ext, halo_out, halo_in, req_out, req_in, req_t, slot_t, unpack, send, recv,
    inverse, adj_z, adj_y, acc, sum_out, sum_in,
    halo_send_sem, halo_recv_sem, req_send_sem, req_recv_sem, line_send_sem, line_recv_sem,
    sum_send_sem, sum_recv_sem,
):
    x_rows, depth, lanes = est.shape
    views = obs.shape[0]
    lines = x_rows * depth
    cap = 2 * lines // n
    slots = n * cap
    per_block = lanes // cap
    taps = px.shape[1]
    taps_z = pz.shape[1]
    half = taps // 2
    edge = half * depth
    me = lax.axis_index("tile")

    barrier = pltpu.get_barrier_semaphore()

    @pl.loop(1, n)
    def _(j):
        pl.semaphore_signal(barrier, inc=1, device_id={"tile": lax.rem(me + j, n)}, device_id_type=MESH)

    halo_out[0] = est[0:half].reshape(edge, lanes).astype(BF16)
    halo_out[1] = est[x_rows - half : x_rows].reshape(edge, lanes).astype(BF16)

    wanted = rows[...]
    owner = wanted // x_rows
    line_id = lax.broadcasted_iota(jnp.int32, (views, lines), 1)
    payload = ((wanted - owner * x_rows) * depth + lax.rem(line_id, depth)).astype(F32)
    hits = [jnp.where(owner == o, 1.0, 0.0) for o in range(n)]
    earlier = one_hot(
        lax.broadcasted_iota(jnp.int32, (lines, lines), 0) < lax.broadcasted_iota(jnp.int32, (lines, lines), 1)
    )
    rank = dot(jnp.concatenate(hits, axis=0).astype(BF16), earlier)
    slot = jnp.zeros((views, lines), F32)
    for o in range(n):
        slot = slot + hits[o] * (rank[o * views : (o + 1) * views] + float(o * cap))
    padded = jnp.concatenate([slot, jnp.zeros((lanes - views, lines), F32)], axis=0)
    slot_t[...] = padded.T

    view_row = lax.broadcasted_iota(jnp.int32, (views, lines), 0)
    slot_lane = lax.broadcasted_iota(jnp.int32, (lines, slots), 1).astype(F32)

    def request(v, total):
        column = pltpu.roll(slot_t[...], lax.rem(lanes - v, lanes), 1)[:, 0:1]
        chosen = one_hot(column == slot_lane)
        unpack[v] = chosen
        return total + dot(jnp.where(view_row == v, payload, 0.0).astype(BF16), chosen)

    requests = lax.fori_loop(0, views, request, jnp.zeros((views, slots), F32))
    for b in range(slots // lanes):
        req_out[b] = requests[:, b * lanes : (b + 1) * lanes]

    pl.semaphore_wait(barrier, n - 1)

    def halo_copy(source, target, send_sem, recv_sem, side, device):
        return pltpu.make_async_remote_copy(
            src_ref=source.at[side], dst_ref=target.at[1 - side],
            send_sem=send_sem.at[side], recv_sem=recv_sem.at[1 - side],
            device_id={"tile": device}, device_id_type=MESH,
        )

    def to_prev(source, target, send_sem, recv_sem):
        return halo_copy(source, target, send_sem, recv_sem, 0, lax.rem(me + n - 1, n))

    def to_next(source, target, send_sem, recv_sem):
        return halo_copy(source, target, send_sem, recv_sem, 1, lax.rem(me + 1, n))

    def request_copy(j):
        d = lax.rem(me + j, n)
        return pltpu.make_async_remote_copy(
            src_ref=req_out.at[d // per_block], dst_ref=req_in.at[me],
            send_sem=req_send_sem, recv_sem=req_recv_sem,
            device_id={"tile": d}, device_id_type=MESH,
        )

    @pl.loop(1, n)
    def _(j):
        request_copy(j).start()

    halos = (halo_out, halo_in, halo_send_sem, halo_recv_sem)

    @pl.when(me > 0)
    def _():
        to_prev(*halos).start()

    @pl.when(me < n - 1)
    def _():
        to_next(*halos).start()

    req_in[me] = req_out[me // per_block]
    ahead = pl.ds(0, n - 1)
    pltpu.make_async_copy(req_in.at[ahead], req_in.at[ahead], req_recv_sem).wait()
    pltpu.make_async_copy(req_in.at[ahead], req_in.at[ahead], req_send_sem).wait()

    req_t[...] = req_in[...].reshape(n * views, lanes).T
    mine = req_t[pl.ds(lax.rem(me, per_block) * cap, cap), :]
    line_lane = lax.broadcasted_iota(jnp.int32, (cap, lines), 1).astype(F32)
    own = pl.ds(pl.multiple_of(me * cap, cap), cap)

    @pl.loop(0, views)
    def _(v):
        turned = pltpu.roll(mine, lax.rem(lanes - v, lanes), 1)
        chosen = jnp.concatenate(
            [one_hot(turned[:, d * views : d * views + 1] == line_lane) for d in range(n)], axis=0
        )
        send[v] = dot(chosen, obs[v].reshape(lines, lanes)).astype(BF16)

        @pl.loop(1, n)
        def _(j):
            d = lax.rem(me + j, n)
            pltpu.make_async_remote_copy(
                src_ref=send.at[v, pl.ds(pl.multiple_of(d * cap, cap), cap)], dst_ref=recv.at[v, own],
                send_sem=line_send_sem.at[v], recv_sem=line_recv_sem.at[v],
                device_id={"tile": d}, device_id_type=MESH,
            ).start()

        recv[v, own] = send[v, own]

    ext[half : half + x_rows] = est[...]

    @pl.when(me > 0)
    def _():
        to_prev(*halos).wait_send()
        pltpu.make_async_copy(halo_in.at[0], halo_in.at[0], halo_recv_sem.at[0]).wait()
        ext[0:half] = halo_in[0].astype(F32).reshape(half, depth, lanes)

    @pl.when(me == 0)
    def _():
        ext[0:half] = jnp.zeros((half, depth, lanes), F32)

    @pl.when(me < n - 1)
    def _():
        to_next(*halos).wait_send()
        pltpu.make_async_copy(halo_in.at[1], halo_in.at[1], halo_recv_sem.at[1]).wait()
        ext[half + x_rows :] = halo_in[1].astype(F32).reshape(half, depth, lanes)

    @pl.when(me == n - 1)
    def _():
        ext[half + x_rows :] = jnp.zeros((half, depth, lanes), F32)

    acc[...] = jnp.zeros(acc.shape, F32)
    copies = lanes // depth
    tall = copies * depth
    y_gap = lax.broadcasted_iota(jnp.int32, (lanes, lanes), 0) - lax.broadcasted_iota(jnp.int32, (lanes, lanes), 1)
    z_gap = (
        lax.rem(lax.broadcasted_iota(jnp.int32, (depth, tall), 1), depth)
        - lax.broadcasted_iota(jnp.int32, (depth, tall), 0)
    )
    same_block = (
        lax.broadcasted_iota(jnp.int32, (tall, tall), 0) // depth
        == lax.broadcasted_iota(jnp.int32, (tall, tall), 1) // depth
    )

    def total_of(ref, v, count):
        total = ref[v, 0]
        for k in range(1, count):
            total = total + ref[v, k]
        return total

    @pl.loop(0, views)
    def _(v):
        sum_x, sum_y, sum_z = total_of(px, v, taps), total_of(py, v, taps), total_of(pz, v, taps_z)
        scale_y = 1.0 / jnp.full((1, lanes), sum_y, F32)
        scale_z = 1.0 / jnp.full((1, tall), sum_z * sum_x, F32)
        fwd_y = jnp.zeros((lanes, lanes), F32)
        back_y = jnp.zeros((lanes, lanes), F32)
        for k in range(taps):
            fwd_y = jnp.where(y_gap == k - half, py[v, k], fwd_y)
            back_y = jnp.where(y_gap == half - k, py[v, k], back_y)
        fwd_z = jnp.zeros((depth, tall), F32)
        back_z = jnp.zeros((depth, tall), F32)
        for k in range(taps_z):
            fwd_z = jnp.where(z_gap == k - taps_z // 2, pz[v, k], fwd_z)
            back_z = jnp.where(z_gap == taps_z // 2 - k, pz[v, k], back_z)
        blocks_fwd = jnp.where(same_block, jnp.concatenate([fwd_z * scale_z] * copies, axis=0), 0.0)
        blocks_back = jnp.where(same_block, jnp.concatenate([back_z * scale_z] * copies, axis=0), 0.0)
        adj_z[v, 0], adj_z[v, 1] = split(blocks_back)
        adj_y[v, 0], adj_y[v, 1] = split(back_y * scale_y)
        z_parts = split(blocks_fwd)
        y_parts = split(fwd_y * scale_y)
        along_x = px[v, 0] * ext[0:x_rows]
        for k in range(1, taps):
            along_x = along_x + px[v, k] * ext[k : k + x_rows]
        along_x = along_x.reshape(lines, lanes)
        for part in range(lines // tall):
            piece = dot_split(z_parts, split(along_x[part * tall : (part + 1) * tall]))
            inverse[v, part * tall : (part + 1) * tall] = 1.0 / dot_split(split(piece), y_parts)

    last_lane = lax.broadcasted_iota(jnp.int32, (lines, lanes), 1) == lanes - 1
    arrived = pl.ds(0, slots - cap)

    @pl.loop(0, views)
    def _(v):
        pltpu.make_async_copy(recv.at[v, arrived], recv.at[v, arrived], line_recv_sem.at[v]).wait()
        line = dot(unpack[v], recv[v])
        following = jnp.where(last_lane, line, pltpu.roll(line, lanes - 1, 1))
        weight = interp[v].reshape(lines, lanes).astype(F32)
        quotient = (weight * line + (1.0 - weight) * following) * inverse[v]
        along_y = dot_split(split(quotient), (adj_y[v, 0], adj_y[v, 1]))
        z_parts = (adj_z[v, 0], adj_z[v, 1])
        corrected = jnp.concatenate(
            [dot_split(z_parts, split(along_y[p * tall : (p + 1) * tall])) for p in range(lines // tall)], axis=0
        ).reshape(x_rows, depth, lanes)
        for r in range(x_rows + 2 * half):
            total = acc[r]
            for k in range(taps):
                if 0 <= r - k < x_rows:
                    total = total + px[v, k] * corrected[r - k]
            acc[r] = total

    sum_out[0] = acc[0:half].reshape(edge, lanes).astype(BF16)
    sum_out[1] = acc[half + x_rows :].reshape(edge, lanes).astype(BF16)
    sums = (sum_out, sum_in, sum_send_sem, sum_recv_sem)

    @pl.when(me > 0)
    def _():
        to_prev(*sums).start()

    @pl.when(me < n - 1)
    def _():
        to_next(*sums).start()

    @pl.loop(0, views)
    def _(v):
        pltpu.make_async_copy(send.at[v, arrived], send.at[v, arrived], line_send_sem.at[v]).wait()

    out[...] = acc[half : half + x_rows]

    @pl.when(me > 0)
    def _():
        to_prev(*sums).wait_send()
        pltpu.make_async_copy(sum_in.at[0], sum_in.at[0], sum_recv_sem.at[0]).wait()
        out[0:half] = out[0:half] + sum_in[0].astype(F32).reshape(half, depth, lanes)

    @pl.when(me < n - 1)
    def _():
        to_next(*sums).wait_send()
        pltpu.make_async_copy(sum_in.at[1], sum_in.at[1], sum_recv_sem.at[1]).wait()
        out[x_rows - half :] = out[x_rows - half :] + sum_in[1].astype(F32).reshape(half, depth, lanes)


def body(estimate, observed, interp, source_rows, tissue, psf_x, psf_y, psf_z):
    n = lax.axis_size("tile")
    x_rows, depth, lanes = estimate.shape
    views = observed.shape[0]
    lines = x_rows * depth
    cap = 2 * lines // n
    slots = n * cap
    taps = psf_x.shape[1]
    half = taps // 2
    if cap % 16 or lanes % cap or n * views != lanes:
        return body_by_collectives(estimate, observed, interp, source_rows, tissue, psf_x, psf_y, psf_z)
    vmem = pl.BlockSpec(memory_space=pltpu.VMEM)
    smem = pl.BlockSpec(memory_space=pltpu.SMEM)
    edge = (2, half * depth, lanes)
    dma = pltpu.SemaphoreType.DMA
    running = pl.pallas_call(
        functools.partial(sweep_kernel, n),
        out_shape=jax.ShapeDtypeStruct(estimate.shape, F32),
        in_specs=[vmem] * 4 + [smem] * 3,
        out_specs=vmem,
        scratch_shapes=[
            pltpu.VMEM((x_rows + 2 * half, depth, lanes), F32),
            pltpu.VMEM(edge, BF16),
            pltpu.VMEM(edge, BF16),
            pltpu.VMEM((slots // lanes, views, lanes), F32),
            pltpu.VMEM((n, views, lanes), F32),
            pltpu.VMEM((lanes, n * views), F32),
            pltpu.VMEM((lines, lanes), F32),
            pltpu.VMEM((views, lines, slots), BF16),
            pltpu.VMEM((views, slots, lanes), BF16),
            pltpu.VMEM((views, slots, lanes), BF16),
            pltpu.VMEM((views, lines, lanes), F32),
            pltpu.VMEM((views, 2, lanes, lanes), BF16),
            pltpu.VMEM((views, 2, lanes, lanes), BF16),
            pltpu.VMEM((x_rows + 2 * half, depth, lanes), F32),
            pltpu.VMEM(edge, BF16),
            pltpu.VMEM(edge, BF16),
            dma((2,)), dma((2,)), dma, dma, dma((views,)), dma((views,)), dma((2,)), dma((2,)),
        ],
        compiler_params=pltpu.CompilerParams(
            collective_id=0, has_side_effects=True, vmem_limit_bytes=40 * 1024 * 1024
        ),
    )(estimate, observed, interp, source_rows.reshape(views, lines), psf_x, psf_y, psf_z)
    updated = estimate * running / views
    return jnp.where(tissue[:, None, None] == 1, updated, estimate)


def solution(mesh):
    return jax.shard_map(
        body,
        mesh=mesh,
        in_specs=(
            P(("slab", "tile"), None, None),
            P(None, ("slab", "tile"), None, None),
            P(None, ("slab", "tile"), None, None),
            P(None, ("slab", "tile"), None),
            P(("slab", "tile")),
            P(),
            P(),
            P(),
        ),
        out_specs=P(("slab", "tile"), None, None),
        check_vma=False,
    )
```

profile of v0, /device:TPU:1, one launch (start us, length us, event | category | flops | bytes accessed | tf_op | source)
XLA Modules:
  0.0 44.1 jit_solution(4378530916442831622)
XLA Ops:
  0.0 0.0 copy-start.3
  0.0 0.0 copy-start.4
  0.0 0.0 copy-start.5
  0.0 0.9 %reshape.5.rows = s32[8,256]{1,0:T(8,128)S(1)} reshape(s32[8,8,32]{2,1,0:T(8,128)} %param.11) | data formatting | bytes 16384 | tf_op jit(solution)/shard_map/reshape | solution.py:423
  0.9 0.0 copy-done.3
  0.9 0.0 copy-done.4
  0.9 0.0 copy-done.5
  0.9 0.0 copy-start
  0.9 1.0 %copy-done = bf16[8,8,32,128]{3,2,1,0:T(8,128)(2,1)S(1)} copy-done((bf16[8,8,32,128]{3,2,1,0:T(8,128)(2,1)S(1)}, bf16[8,8,32,128]{3,2,1,0:T(8,128)(2,1)}, u32[]{:S(2)}) %copy-start) | copy-done | bytes 524312
  1.9 0.0 copy-start.1
  1.9 1.0 %copy-done.1 = bf16[8,8,32,128]{3,2,1,0:T(8,128)(2,1)S(1)} copy-done((bf16[8,8,32,128]{3,2,1,0:T(8,128)(2,1)S(1)}, bf16[8,8,32,128]{3,2,1,0:T(8,128)(2,1)}, u32[]{:S(2)}) %copy-start.1) | copy-done | bytes 524312
  3.0 0.0 copy-start.2
  3.0 0.9 %copy-done.2 = f32[8,32,128]{2,1,0:T(8,128)S(1)} copy-done((f32[8,32,128]{2,1,0:T(8,128)S(1)}, f32[8,32,128]{2,1,0:T(8,128)}, u32[]{:S(2)}) %copy-start.2) | copy-done | bytes 131096
  3.9 0.0 copy-start.6
  3.9 39.5 %shard_map.82 = f32[8,32,128]{2,1,0:T(8,128)S(1)} custom-call(f32[8,32,128]{2,1,0:T(8,128)S(1)} %copy-done.2, bf16[8,8,32,128]{3,2,1,0:T(8,128)(2,1)S(1)} %copy-done, bf16[8,8,32,128]{3,2,1,0:T(8,128)(2,1)S(1)} %copy-done.1, s32[8,256]{1,0:T(8,128)S(1)} %reshape.5.rows, f32[8,9]{1,0:T(8,128)S(1)} %copy-done.3, f32[8,9]{1,0:T(8,128)S(1)} %copy-done.4, ...), custom_call_target="tpu_custom_call" | custom-call | tf_op jit(solution)/shard_map/pallas_call | solution.py:396
  43.4 0.0 copy-done.6
  43.4 0.7 %multiply_select_fusion = f32[8,32,128]{2,1,0:T(8,128)} fusion(f32[8,32,128]{2,1,0:T(8,128)S(1)} %copy-done.2, f32[8,32,128]{2,1,0:T(8,128)S(1)} %shard_map.82, pred[8]{0:T(512)(128)(4,1)S(1)} %broadcast_compare_fusion), kind=kLoop, calls=%fused_computation | loop fusion | flops 98304 | bytes 393224 | tf_op jit(solution)/shard_map/jit(_where)/select_n | solution.py:425
  (1 shorter events, 0.0 us)
Async XLA Ops:
  0.0 0.9 %copy-start.3 = (f32[8,9]{1,0:T(8,128)S(1)}, f32[8,9]{1,0:T(8,128)}, u32[]{:S(2)}) copy-start(f32[8,9]{1,0:T(8,128)} %px.1) | copy-start | bytes 868
  0.0 0.9 %copy-start.4 = (f32[8,9]{1,0:T(8,128)S(1)}, f32[8,9]{1,0:T(8,128)}, u32[]{:S(2)}) copy-start(f32[8,9]{1,0:T(8,128)} %py.1) | copy-start | bytes 868
  0.0 0.9 %copy-start.5 = (f32[8,33]{1,0:T(8,128)S(1)}, f32[8,33]{1,0:T(8,128)}, u32[]{:S(2)}) copy-start(f32[8,33]{1,0:T(8,128)} %pz.1) | copy-start | bytes 3172
  0.9 1.0 %copy-start = (bf16[8,8,32,128]{3,2,1,0:T(8,128)(2,1)S(1)}, bf16[8,8,32,128]{3,2,1,0:T(8,128)(2,1)}, u32[]{:S(2)}) copy-start(bf16[8,8,32,128]{3,2,1,0:T(8,128)(2,1)} %obs.1) | copy-start | bytes 1572868
  1.9 1.0 %copy-start.1 = (bf16[8,8,32,128]{3,2,1,0:T(8,128)(2,1)S(1)}, bf16[8,8,32,128]{3,2,1,0:T(8,128)(2,1)}, u32[]{:S(2)}) copy-start(bf16[8,8,32,128]{3,2,1,0:T(8,128)(2,1)} %interp.1) | copy-start | bytes 1572868
  3.0 0.9 %copy-start.2 = (f32[8,32,128]{2,1,0:T(8,128)S(1)}, f32[8,32,128]{2,1,0:T(8,128)}, u32[]{:S(2)}) copy-start(f32[8,32,128]{2,1,0:T(8,128)} %est.1) | copy-start | bytes 393220
  3.9 39.5 %copy-start.6 = (s32[8]{0:T(128)S(1)}, s32[8]{0:T(128)}, u32[]{:S(2)}) copy-start(s32[8]{0:T(128)} %param.12) | copy-start | bytes 100
where the time goes:
time: 44.4 us; the launch traced here: 44.1 us
  Pallas kernels  39.5 us (89%)
  local copies, waits for them, and re-layouts  3.87 us (9%)
  other arithmetic  0.74 us (2%)
    pallas_call x1, Pallas kernels, body(): pl.pallas_call(functools.partial(sweep_kernel, n), out_shape=jax.ShapeDty...  39.5 us
    unnamed x14, local copies, waits for them, and re-layouts  3 us

commit v1 on v0

--- a/solution.py
+++ b/solution.py
@@ -112,6 +112,7 @@
 
 
 MESH = pl.DeviceIdType.MESH
+RELAY_AFTER = 3
 F32 = jnp.float32
 BF16 = jnp.bfloat16
 
@@ -134,11 +135,12 @@
 
 
 def sweep_kernel(
-    n, est, obs, interp, rows, px, py, pz, out,
-    ext, halo_out, halo_in, req_out, req_in, req_t, slot_t, unpack, send, recv,
+    n, est_far, obs_far, interp_far, rows_far, tissue_far, px_far, py_far, pz_far, out,
+    est, obs, interp, rows, tissue, px, py, pz, in_sem,
+    ext, halo_out, halo_in, req_out, req_in, req_t, relay_in, relay_t, raw, raw_send, slot_t, unpack, send, recv,
     inverse, adj_z, adj_y, acc, sum_out, sum_in,
     halo_send_sem, halo_recv_sem, req_send_sem, req_recv_sem, line_send_sem, line_recv_sem,
-    sum_send_sem, sum_recv_sem,
+    sum_send_sem, sum_recv_sem, relay_send_sem, relay_recv_sem, raw_send_sem, raw_recv_sem,
 ):
     x_rows, depth, lanes = est.shape
     views = obs.shape[0]
@@ -151,17 +153,27 @@
     half = taps // 2
     edge = half * depth
     me = lax.axis_index("tile")
+    side = n // 2
+    place = lax.rem(me, side)
+    base = me - place
+    partner = lax.rem(me + side, n)
+    partner_base = partner - place
 
     barrier = pltpu.get_barrier_semaphore()
+    pairs = (
+        (rows_far, rows), (est_far, est), (obs_far, obs), (interp_far, interp), (px_far, px), (py_far, py), (pz_far, pz),
+        (tissue_far, tissue),
+    )
+    loads = [pltpu.make_async_copy(far, near, in_sem.at[i]) for i, (far, near) in enumerate(pairs)]
+    for load in loads:
+        load.start()
 
     @pl.loop(1, n)
     def _(j):
         pl.semaphore_signal(barrier, inc=1, device_id={"tile": lax.rem(me + j, n)}, device_id_type=MESH)
 
-    halo_out[0] = est[0:half].reshape(edge, lanes).astype(BF16)
-    halo_out[1] = est[x_rows - half : x_rows].reshape(edge, lanes).astype(BF16)
-
-    wanted = rows[...]
+    loads[0].wait()
+    wanted = jnp.concatenate([rows[:, x, :] for x in range(x_rows)], axis=1)
     owner = wanted // x_rows
     line_id = lax.broadcasted_iota(jnp.int32, (views, lines), 1)
     payload = ((wanted - owner * x_rows) * depth + lax.rem(line_id, depth)).astype(F32)
@@ -189,6 +201,10 @@
     for b in range(slots // lanes):
         req_out[b] = requests[:, b * lanes : (b + 1) * lanes]
 
+    loads[1].wait()
+    halo_out[0] = est[0:half].reshape(edge, lanes).astype(BF16)
+    halo_out[1] = est[x_rows - half : x_rows].reshape(edge, lanes).astype(BF16)
+    loads[2].wait()
     pl.semaphore_wait(barrier, n - 1)
 
     def halo_copy(source, target, send_sem, recv_sem, side, device):
@@ -212,9 +228,28 @@
             device_id={"tile": d}, device_id_type=MESH,
         )
 
+    def relay_request_copy(j):
+        d = base + lax.rem(place + j, side)
+        return pltpu.make_async_remote_copy(
+            src_ref=req_out.at[lax.rem(d + side, n) // per_block], dst_ref=relay_in.at[place],
+            send_sem=relay_send_sem, recv_sem=relay_recv_sem,
+            device_id={"tile": d}, device_id_type=MESH,
+        )
+
+    raw_copy = pltpu.make_async_remote_copy(
+        src_ref=obs.at[0], dst_ref=raw, send_sem=raw_send_sem, recv_sem=raw_recv_sem,
+        device_id={"tile": partner}, device_id_type=MESH,
+    )
+
     @pl.loop(1, n)
     def _(j):
         request_copy(j).start()
+
+    raw_copy.start()
+
+    @pl.loop(1, side)
+    def _(j):
+        relay_request_copy(j).start()
 
     halos = (halo_out, halo_in, halo_send_sem, halo_recv_sem)
 
@@ -236,24 +271,61 @@
     line_lane = lax.broadcasted_iota(jnp.int32, (cap, lines), 1).astype(F32)
     own = pl.ds(pl.multiple_of(me * cap, cap), cap)
 
-    @pl.loop(0, views)
-    def _(v):
+    def line_copy(v, source, target, d):
+        return pltpu.make_async_remote_copy(
+            src_ref=source, dst_ref=recv.at[v, target],
+            send_sem=line_send_sem.at[v], recv_sem=line_recv_sem.at[v],
+            device_id={"tile": d}, device_id_type=MESH,
+        )
+
+    def chunk(index):
+        return pl.ds(pl.multiple_of(index * cap, cap), cap)
+
+    def pack(v):
         turned = pltpu.roll(mine, lax.rem(lanes - v, lanes), 1)
         chosen = jnp.concatenate(
             [one_hot(turned[:, d * views : d * views + 1] == line_lane) for d in range(n)], axis=0
         )
         send[v] = dot(chosen, obs[v].reshape(lines, lanes)).astype(BF16)
 
-        @pl.loop(1, n)
+    def send_view(v):
+        pack(v)
+
+        @pl.loop(0, side)
         def _(j):
-            d = lax.rem(me + j, n)
-            pltpu.make_async_remote_copy(
-                src_ref=send.at[v, pl.ds(pl.multiple_of(d * cap, cap), cap)], dst_ref=recv.at[v, own],
-                send_sem=line_send_sem.at[v], recv_sem=line_recv_sem.at[v],
-                device_id={"tile": d}, device_id_type=MESH,
-            ).start()
+            d = partner_base + lax.rem(place + j, side)
+            line_copy(v, send.at[v, chunk(d)], own, d).start()
+
+        @pl.loop(1, side)
+        def _(j):
+            d = base + lax.rem(place + j, side)
+            line_copy(v, send.at[v, chunk(d)], own, d).start()
 
         recv[v, own] = send[v, own]
+
+    pl.loop(1, RELAY_AFTER)(send_view)
+
+    pltpu.make_async_copy(relay_in.at[pl.ds(0, side - 1)], relay_in.at[pl.ds(0, side - 1)], relay_recv_sem).wait()
+    pltpu.make_async_copy(relay_in.at[pl.ds(0, side - 1)], relay_in.at[pl.ds(0, side - 1)], relay_send_sem).wait()
+    relay_in[place] = req_out[partner // per_block]
+    relay_t[...] = relay_in[...].reshape(side * views, lanes).T
+    others = relay_t[pl.ds(lax.rem(partner, per_block) * cap, cap), :]
+    chosen_raw = jnp.concatenate(
+        [one_hot(others[:, d * views : d * views + 1] == line_lane) for d in range(side)], axis=0
+    )
+    pack(0)
+    raw_copy.wait()
+    raw_send[...] = dot(chosen_raw, raw[...].reshape(lines, lanes)).astype(BF16)
+
+    @pl.loop(1, side)
+    def _(j):
+        there = lax.rem(place + j, side)
+        line_copy(0, raw_send.at[chunk(there)], chunk(partner), base + there).start()
+        line_copy(0, send.at[0, chunk(base + there)], own, base + there).start()
+
+    recv[0, own] = send[0, own]
+    recv[0, chunk(partner)] = raw_send[chunk(place)]
+    pl.loop(RELAY_AFTER, views)(send_view)
 
     ext[half : half + x_rows] = est[...]
 
@@ -277,6 +349,8 @@
     def _():
         ext[half + x_rows :] = jnp.zeros((half, depth, lanes), F32)
 
+    for load in loads[3:]:
+        load.wait()
     acc[...] = jnp.zeros(acc.shape, F32)
     copies = lanes // depth
     tall = copies * depth
@@ -328,9 +402,20 @@
     last_lane = lax.broadcasted_iota(jnp.int32, (lines, lanes), 1) == lanes - 1
     arrived = pl.ds(0, slots - cap)
 
+    relayed = pl.ds(0, 2 * (side - 1) * cap)
+
     @pl.loop(0, views)
-    def _(v):
-        pltpu.make_async_copy(recv.at[v, arrived], recv.at[v, arrived], line_recv_sem.at[v]).wait()
+    def _(turn):
+        v = jnp.where(turn < RELAY_AFTER - 1, turn + 1, jnp.where(turn == RELAY_AFTER - 1, 0, turn))
+
+        @pl.when(v == 0)
+        def _():
+            pltpu.make_async_copy(recv.at[0, relayed], recv.at[0, relayed], line_recv_sem.at[0]).wait()
+
+        @pl.when(v > 0)
+        def _():
+            pltpu.make_async_copy(recv.at[v, arrived], recv.at[v, arrived], line_recv_sem.at[v]).wait()
+
         line = dot(unpack[v], recv[v])
         following = jnp.where(last_lane, line, pltpu.roll(line, lanes - 1, 1))
         weight = interp[v].reshape(lines, lanes).astype(F32)
@@ -359,23 +444,27 @@
     def _():
         to_next(*sums).start()
 
-    @pl.loop(0, views)
+    pltpu.make_async_copy(send.at[0, relayed], send.at[0, relayed], line_send_sem.at[0]).wait()
+
+    @pl.loop(1, views)
     def _(v):
         pltpu.make_async_copy(send.at[v, arrived], send.at[v, arrived], line_send_sem.at[v]).wait()
 
-    out[...] = acc[half : half + x_rows]
-
     @pl.when(me > 0)
     def _():
         to_prev(*sums).wait_send()
         pltpu.make_async_copy(sum_in.at[0], sum_in.at[0], sum_recv_sem.at[0]).wait()
-        out[0:half] = out[0:half] + sum_in[0].astype(F32).reshape(half, depth, lanes)
+        acc[half : 2 * half] = acc[half : 2 * half] + sum_in[0].astype(F32).reshape(half, depth, lanes)
 
     @pl.when(me < n - 1)
     def _():
         to_next(*sums).wait_send()
         pltpu.make_async_copy(sum_in.at[1], sum_in.at[1], sum_recv_sem.at[1]).wait()
-        out[x_rows - half :] = out[x_rows - half :] + sum_in[1].astype(F32).reshape(half, depth, lanes)
+        acc[x_rows : x_rows + half] = acc[x_rows : x_rows + half] + sum_in[1].astype(F32).reshape(half, depth, lanes)
+
+    for x in range(x_rows):
+        updated = est[x] * acc[half + x] * (1.0 / views)
+        out[x] = jnp.where(jnp.full((depth, lanes), tissue[x]) == 1, updated, est[x])
 
 
 def body(estimate, observed, interp, source_rows, tissue, psf_x, psf_y, psf_z):
@@ -390,21 +479,33 @@
     if cap % 16 or lanes % cap or n * views != lanes:
         return body_by_collectives(estimate, observed, interp, source_rows, tissue, psf_x, psf_y, psf_z)
     vmem = pl.BlockSpec(memory_space=pltpu.VMEM)
-    smem = pl.BlockSpec(memory_space=pltpu.SMEM)
     edge = (2, half * depth, lanes)
     dma = pltpu.SemaphoreType.DMA
-    running = pl.pallas_call(
+    return pl.pallas_call(
         functools.partial(sweep_kernel, n),
         out_shape=jax.ShapeDtypeStruct(estimate.shape, F32),
-        in_specs=[vmem] * 4 + [smem] * 3,
+        in_specs=[pl.BlockSpec(memory_space=pl.ANY)] * 8,
         out_specs=vmem,
         scratch_shapes=[
+            pltpu.VMEM(estimate.shape, F32),
+            pltpu.VMEM(observed.shape, BF16),
+            pltpu.VMEM(interp.shape, BF16),
+            pltpu.VMEM(source_rows.shape, jnp.int32),
+            pltpu.SMEM(tissue.shape, jnp.int32),
+            pltpu.SMEM(psf_x.shape, F32),
+            pltpu.SMEM(psf_y.shape, F32),
+            pltpu.SMEM(psf_z.shape, F32),
+            dma((8,)),
             pltpu.VMEM((x_rows + 2 * half, depth, lanes), F32),
             pltpu.VMEM(edge, BF16),
             pltpu.VMEM(edge, BF16),
             pltpu.VMEM((slots // lanes, views, lanes), F32),
             pltpu.VMEM((n, views, lanes), F32),
             pltpu.VMEM((lanes, n * views), F32),
+            pltpu.VMEM((n // 2, views, lanes), F32),
+            pltpu.VMEM((lanes, n // 2 * views), F32),
+            pltpu.VMEM((x_rows, depth, lanes), BF16),
+            pltpu.VMEM((n // 2 * cap, lanes), BF16),
             pltpu.VMEM((lines, lanes), F32),
             pltpu.VMEM((views, lines, slots), BF16),
             pltpu.VMEM((views, slots, lanes), BF16),
@@ -415,14 +516,12 @@
             pltpu.VMEM((x_rows + 2 * half, depth, lanes), F32),
             pltpu.VMEM(edge, BF16),
             pltpu.VMEM(edge, BF16),
-            dma((2,)), dma((2,)), dma, dma, dma((views,)), dma((views,)), dma((2,)), dma((2,)),
+            dma((2,)), dma((2,)), dma, dma, dma((views,)), dma((views,)), dma((2,)), dma((2,)), dma, dma, dma, dma,
         ],
         compiler_params=pltpu.CompilerParams(
-            collective_id=0, has_side_effects=True, vmem_limit_bytes=40 * 1024 * 1024
+            collective_id=0, has_side_effects=True, vmem_limit_bytes=60 * 1024 * 1024
         ),
-    )(estimate, observed, interp, source_rows.reshape(views, lines), psf_x, psf_y, psf_z)
-    updated = estimate * running / views
-    return jnp.where(tissue[:, None, None] == 1, updated, estimate)
+    )(estimate, observed, interp, source_rows, tissue, psf_x, psf_y, psf_z)
 
 
 def solution(mesh):

time: 44.4 us -> 39.3 us (0.89)
  local copies, waits for them, and re-layouts: 3.87 us -> 1.57 us
  Pallas kernels: 39.5 us -> 37.6 us
  other arithmetic: 0.74 us -> 0 us
    pallas_call x1, Pallas kernels: 39.5 us -> 37.6 us  [body(): pl.pallas_call(functools.partial(sweep_kernel, n), out_shape=jax.ShapeDty...]
    unnamed x14 -> x1, local copies, waits for them, and re-layouts: 3 us -> 1.57 us
    reshape x1 -> x0, local copies, waits for them, and re-layouts: 0.87 us -> none  [body(): source_rows.reshape(views, lines)]
    select_n x1 -> x0, other arithmetic: 0.73 us -> none  [body(): return jnp.where(tissue[:, None, None] == 1, updated, estimate)]
where the time goes in v1:
time: 39.3 us; the launch traced here: 39.1 us
  Pallas kernels  37.6 us (96%)
  local copies, waits for them, and re-layouts  1.57 us (4%)
    pallas_call x1, Pallas kernels, body(): pl.pallas_call(functools.partial(sweep_kernel, n), out_shape=jax.ShapeDty...  37.6 us
    unnamed x1, local copies, waits for them, and re-layouts  1.57 us

profile of v1, /device:TPU:1, one launch (start us, length us, event | category | flops | bytes accessed | tf_op | source)
XLA Modules:
  0.0 39.1 jit_solution(12497921029370098044)
XLA Ops:
  0.0 37.6 %shard_map.82 = f32[8,32,128]{2,1,0:T(8,128)} custom-call(f32[8,32,128]{2,1,0:T(8,128)} %est_far.1, bf16[8,8,32,128]{3,2,1,0:T(8,128)(2,1)} %obs_far.1, bf16[8,8,32,128]{3,2,1,0:T(8,128)(2,1)} %interp_far.1, s32[8,8,32]{2,1,0:T(8,128)} %rows_far.1, s32[8]{0:T(128)} %tissue_far.1, f32[8,9]{1,0:T(8,128)} %px_far.1, f32[8,9]{1,0:T(8,128)} %py_far.1, f32[8,33]{1,0:T(8,128)} %pz_far.1), custom_call_target="tpu_custom_call" | custom-call | tf_op jit(solution)/shard_map/pallas_call | solution.py:484
  37.6 1.6 %copy.10 = f32[8,32,128]{2,1,0:T(8,128)} copy(f32[8,32,128]{2,1,0:T(8,128)} %shard_map.82) | data formatting | bytes 262144

commit v2 on v1

--- a/solution.py
+++ b/solution.py
@@ -148,6 +148,7 @@
     cap = 2 * lines // n
     slots = n * cap
     per_block = lanes // cap
+    groups = views // per_block
     taps = px.shape[1]
     taps_z = pz.shape[1]
     half = taps // 2
@@ -181,25 +182,24 @@
     earlier = one_hot(
         lax.broadcasted_iota(jnp.int32, (lines, lines), 0) < lax.broadcasted_iota(jnp.int32, (lines, lines), 1)
     )
-    rank = dot(jnp.concatenate(hits, axis=0).astype(BF16), earlier)
-    slot = jnp.zeros((views, lines), F32)
+    ranks = dot(jnp.concatenate(hits, axis=0).astype(BF16), earlier)
+    rank = jnp.zeros((views, lines), F32)
+    offset = jnp.zeros((views, lines), F32)
     for o in range(n):
-        slot = slot + hits[o] * (rank[o * views : (o + 1) * views] + float(o * cap))
-    padded = jnp.concatenate([slot, jnp.zeros((lanes - views, lines), F32)], axis=0)
-    slot_t[...] = padded.T
-
-    view_row = lax.broadcasted_iota(jnp.int32, (views, lines), 0)
-    slot_lane = lax.broadcasted_iota(jnp.int32, (lines, slots), 1).astype(F32)
-
-    def request(v, total):
-        column = pltpu.roll(slot_t[...], lax.rem(lanes - v, lanes), 1)[:, 0:1]
-        chosen = one_hot(column == slot_lane)
-        unpack[v] = chosen
-        return total + dot(jnp.where(view_row == v, payload, 0.0).astype(BF16), chosen)
-
-    requests = lax.fori_loop(0, views, request, jnp.zeros((views, slots), F32))
-    for b in range(slots // lanes):
-        req_out[b] = requests[:, b * lanes : (b + 1) * lanes]
+        rank = rank + hits[o] * ranks[o * views : (o + 1) * views]
+        offset = offset + hits[o] * float(o * cap)
+    spot = rank + (lax.rem(lax.broadcasted_iota(jnp.int32, (views, lines), 0), per_block) * cap).astype(F32)
+    empty = jnp.zeros((lanes - 2 * views, lines), F32)
+    columns = jnp.concatenate([spot, rank + offset, empty], axis=0).T
+    slot_t[...] = columns
+    owner_id = lax.broadcasted_iota(jnp.int32, (n, lines), 0)
+    lane_id = lax.broadcasted_iota(jnp.int32, (lines, lanes), 1).astype(F32)
+    for g in range(groups):
+        total = jnp.zeros((n, lanes), F32)
+        for v in range(g * per_block, (g + 1) * per_block):
+            theirs = jnp.where(owner[v : v + 1] == owner_id, payload[v : v + 1], 0.0).astype(BF16)
+            total = total + dot(theirs, one_hot(columns[:, v : v + 1] == lane_id))
+        req_out[:, g, :] = total
 
     loads[1].wait()
     halo_out[0] = est[0:half].reshape(edge, lanes).astype(BF16)
@@ -223,7 +223,7 @@
     def request_copy(j):
         d = lax.rem(me + j, n)
         return pltpu.make_async_remote_copy(
-            src_ref=req_out.at[d // per_block], dst_ref=req_in.at[me],
+            src_ref=req_out.at[d], dst_ref=req_in.at[me],
             send_sem=req_send_sem, recv_sem=req_recv_sem,
             device_id={"tile": d}, device_id_type=MESH,
         )
@@ -231,7 +231,7 @@
     def relay_request_copy(j):
         d = base + lax.rem(place + j, side)
         return pltpu.make_async_remote_copy(
-            src_ref=req_out.at[lax.rem(d + side, n) // per_block], dst_ref=relay_in.at[place],
+            src_ref=req_out.at[lax.rem(d + side, n)], dst_ref=relay_in.at[place],
             send_sem=relay_send_sem, recv_sem=relay_recv_sem,
             device_id={"tile": d}, device_id_type=MESH,
         )
@@ -261,13 +261,16 @@
     def _():
         to_next(*halos).start()
 
-    req_in[me] = req_out[me // per_block]
+    def turned_requests(ref, count):
+        parts = [ref[:, g, :] for g in range(groups)]
+        return jnp.concatenate(parts + [jnp.zeros((lanes - groups * count, lanes), F32)], axis=0).T
+
+    req_in[me] = req_out[me]
     ahead = pl.ds(0, n - 1)
     pltpu.make_async_copy(req_in.at[ahead], req_in.at[ahead], req_recv_sem).wait()
     pltpu.make_async_copy(req_in.at[ahead], req_in.at[ahead], req_send_sem).wait()
 
-    req_t[...] = req_in[...].reshape(n * views, lanes).T
-    mine = req_t[pl.ds(lax.rem(me, per_block) * cap, cap), :]
+    req_t[...] = turned_requests(req_in, n)
     line_lane = lax.broadcasted_iota(jnp.int32, (cap, lines), 1).astype(F32)
     own = pl.ds(pl.multiple_of(me * cap, cap), cap)
 
@@ -282,10 +285,10 @@
         return pl.ds(pl.multiple_of(index * cap, cap), cap)
 
     def pack(v):
-        turned = pltpu.roll(mine, lax.rem(lanes - v, lanes), 1)
-        chosen = jnp.concatenate(
-            [one_hot(turned[:, d * views : d * views + 1] == line_lane) for d in range(n)], axis=0
-        )
+        group = v // per_block
+        lines_of_view = req_t[pl.ds(pl.multiple_of((v - group * per_block) * cap, cap), cap), :]
+        turned = pltpu.roll(lines_of_view, lax.rem(lanes - group * n, lanes), 1)
+        chosen = jnp.concatenate([one_hot(turned[:, d : d + 1] == line_lane) for d in range(n)], axis=0)
         send[v] = dot(chosen, obs[v].reshape(lines, lanes)).astype(BF16)
 
     def send_view(v):
@@ -307,12 +310,10 @@
 
     pltpu.make_async_copy(relay_in.at[pl.ds(0, side - 1)], relay_in.at[pl.ds(0, side - 1)], relay_recv_sem).wait()
     pltpu.make_async_copy(relay_in.at[pl.ds(0, side - 1)], relay_in.at[pl.ds(0, side - 1)], relay_send_sem).wait()
-    relay_in[place] = req_out[partner // per_block]
-    relay_t[...] = relay_in[...].reshape(side * views, lanes).T
-    others = relay_t[pl.ds(lax.rem(partner, per_block) * cap, cap), :]
-    chosen_raw = jnp.concatenate(
-        [one_hot(others[:, d * views : d * views + 1] == line_lane) for d in range(side)], axis=0
-    )
+    relay_in[place] = req_out[partner]
+    relay_t[...] = turned_requests(relay_in, side)
+    others = relay_t[0:cap, :]
+    chosen_raw = jnp.concatenate([one_hot(others[:, d : d + 1] == line_lane) for d in range(side)], axis=0)
     pack(0)
     raw_copy.wait()
     raw_send[...] = dot(chosen_raw, raw[...].reshape(lines, lanes)).astype(BF16)
@@ -370,8 +371,11 @@
             total = total + ref[v, k]
         return total
 
+    slot_lane = lax.broadcasted_iota(jnp.int32, (lines, slots), 1).astype(F32)
+
     @pl.loop(0, views)
     def _(v):
+        unpack[v] = one_hot(pltpu.roll(slot_t[...], lax.rem(lanes - views - v, lanes), 1)[:, 0:1] == slot_lane)
         sum_x, sum_y, sum_z = total_of(px, v, taps), total_of(py, v, taps), total_of(pz, v, taps_z)
         scale_y = 1.0 / jnp.full((1, lanes), sum_y, F32)
         scale_z = 1.0 / jnp.full((1, tall), sum_z * sum_x, F32)
@@ -476,7 +480,7 @@
     slots = n * cap
     taps = psf_x.shape[1]
     half = taps // 2
-    if cap % 16 or lanes % cap or n * views != lanes:
+    if cap % 16 or lanes % cap or n * views != lanes or n % 2 or views * cap % lanes:
         return body_by_collectives(estimate, observed, interp, source_rows, tissue, psf_x, psf_y, psf_z)
     vmem = pl.BlockSpec(memory_space=pltpu.VMEM)
     edge = (2, half * depth, lanes)
@@ -499,11 +503,11 @@
             pltpu.VMEM((x_rows + 2 * half, depth, lanes), F32),
             pltpu.VMEM(edge, BF16),
             pltpu.VMEM(edge, BF16),
-            pltpu.VMEM((slots // lanes, views, lanes), F32),
-            pltpu.VMEM((n, views, lanes), F32),
-            pltpu.VMEM((lanes, n * views), F32),
-            pltpu.VMEM((n // 2, views, lanes), F32),
-            pltpu.VMEM((lanes, n // 2 * views), F32),
+            pltpu.VMEM((n, views * cap // lanes, lanes), F32),
+            pltpu.VMEM((n, views * cap // lanes, lanes), F32),
+            pltpu.VMEM((lanes, lanes), F32),
+            pltpu.VMEM((n // 2, views * cap // lanes, lanes), F32),
+            pltpu.VMEM((lanes, lanes), F32),
             pltpu.VMEM((x_rows, depth, lanes), BF16),
             pltpu.VMEM((n // 2 * cap, lanes), BF16),
             pltpu.VMEM((lines, lanes), F32),

time: 39.3 us -> 37.4 us (0.952)
  Pallas kernels: 37.6 us -> 35.7 us
    pallas_call x1, Pallas kernels: 37.6 us -> 35.7 us  [body(): pl.pallas_call(functools.partial(sweep_kernel, n), out_shape=jax.ShapeDty...]
where the time goes in v2:
time: 37.4 us; the launch traced here: 37.3 us
  Pallas kernels  35.7 us (95%)
  local copies, waits for them, and re-layouts  1.57 us (4%)
    pallas_call x1, Pallas kernels, body(): pl.pallas_call(functools.partial(sweep_kernel, n), out_shape=jax.ShapeDty...  35.7 us
    unnamed x1, local copies, waits for them, and re-layouts  1.57 us

profile of v2, /device:TPU:1, one launch (start us, length us, event | category | flops | bytes accessed | tf_op | source)
XLA Modules:
  0.0 37.3 jit_solution(16499177906413289936)
XLA Ops:
  0.0 35.7 %shard_map.82 = f32[8,32,128]{2,1,0:T(8,128)} custom-call(f32[8,32,128]{2,1,0:T(8,128)} %est_far.1, bf16[8,8,32,128]{3,2,1,0:T(8,128)(2,1)} %obs_far.1, bf16[8,8,32,128]{3,2,1,0:T(8,128)(2,1)} %interp_far.1, s32[8,8,32]{2,1,0:T(8,128)} %rows_far.1, s32[8]{0:T(128)} %tissue_far.1, f32[8,9]{1,0:T(8,128)} %px_far.1, f32[8,9]{1,0:T(8,128)} %py_far.1, f32[8,33]{1,0:T(8,128)} %pz_far.1), custom_call_target="tpu_custom_call" | custom-call | tf_op jit(solution)/shard_map/pallas_call | solution.py:488
  35.7 1.6 %copy.10 = f32[8,32,128]{2,1,0:T(8,128)} copy(f32[8,32,128]{2,1,0:T(8,128)} %shard_map.82) | data formatting | bytes 262144

commit v3 on v2

--- a/solution.py
+++ b/solution.py
@@ -245,11 +245,11 @@
     def _(j):
         request_copy(j).start()
 
-    raw_copy.start()
-
     @pl.loop(1, side)
     def _(j):
         relay_request_copy(j).start()
+
+    raw_copy.start()
 
     halos = (halo_out, halo_in, halo_send_sem, halo_recv_sem)
 
@@ -406,6 +406,7 @@
     last_lane = lax.broadcasted_iota(jnp.int32, (lines, lanes), 1) == lanes - 1
     arrived = pl.ds(0, slots - cap)
 
+    sums = (sum_out, sum_in, sum_send_sem, sum_recv_sem)
     relayed = pl.ds(0, 2 * (side - 1) * cap)
 
     @pl.loop(0, views)
@@ -429,24 +430,33 @@
         corrected = jnp.concatenate(
             [dot_split(z_parts, split(along_y[p * tall : (p + 1) * tall])) for p in range(lines // tall)], axis=0
         ).reshape(x_rows, depth, lanes)
-        for r in range(x_rows + 2 * half):
+
+        def add_row(r):
             total = acc[r]
             for k in range(taps):
                 if 0 <= r - k < x_rows:
                     total = total + px[v, k] * corrected[r - k]
             acc[r] = total
 
-    sum_out[0] = acc[0:half].reshape(edge, lanes).astype(BF16)
-    sum_out[1] = acc[half + x_rows :].reshape(edge, lanes).astype(BF16)
-    sums = (sum_out, sum_in, sum_send_sem, sum_recv_sem)
-
-    @pl.when(me > 0)
-    def _():
-        to_prev(*sums).start()
-
-    @pl.when(me < n - 1)
-    def _():
-        to_next(*sums).start()
+        for r in [*range(half), *range(half + x_rows, x_rows + 2 * half)]:
+            add_row(r)
+
+        @pl.when(turn == views - 1)
+        def _():
+            sum_out[0] = acc[0:half].reshape(edge, lanes).astype(BF16)
+            sum_out[1] = acc[half + x_rows :].reshape(edge, lanes).astype(BF16)
+
+            @pl.when(me > 0)
+            def _():
+                to_prev(*sums).start()
+
+            @pl.when(me < n - 1)
+            def _():
+                to_next(*sums).start()
+
+        for r in range(half, half + x_rows):
+            add_row(r)
+
 
     pltpu.make_async_copy(send.at[0, relayed], send.at[0, relayed], line_send_sem.at[0]).wait()
 

time: 37.4 us -> 37.4 us (level)
  no operation moved by 1% of the time
where the time goes in v3:
time: 37.4 us; the launch traced here: 37.2 us
  Pallas kernels  35.7 us (95%)
  local copies, waits for them, and re-layouts  1.57 us (4%)
    pallas_call x1, Pallas kernels, body(): pl.pallas_call(functools.partial(sweep_kernel, n), out_shape=jax.ShapeDty...  35.7 us
    unnamed x1, local copies, waits for them, and re-layouts  1.57 us

profile of v3, /device:TPU:1, one launch (start us, length us, event | category | flops | bytes accessed | tf_op | source)
XLA Modules:
  0.0 37.2 jit_solution(6890649776960961844)
XLA Ops:
  0.0 35.7 %shard_map.82 = f32[8,32,128]{2,1,0:T(8,128)} custom-call(f32[8,32,128]{2,1,0:T(8,128)} %est_far.1, bf16[8,8,32,128]{3,2,1,0:T(8,128)(2,1)} %obs_far.1, bf16[8,8,32,128]{3,2,1,0:T(8,128)(2,1)} %interp_far.1, s32[8,8,32]{2,1,0:T(8,128)} %rows_far.1, s32[8]{0:T(128)} %tissue_far.1, f32[8,9]{1,0:T(8,128)} %px_far.1, f32[8,9]{1,0:T(8,128)} %py_far.1, f32[8,33]{1,0:T(8,128)} %pz_far.1), custom_call_target="tpu_custom_call" | custom-call | tf_op jit(solution)/shard_map/pallas_call | solution.py:498
  35.7 1.6 %copy.10 = f32[8,32,128]{2,1,0:T(8,128)} copy(f32[8,32,128]{2,1,0:T(8,128)} %shard_map.82) | data formatting | bytes 262144
